TPU v7x, 256 devices: a whole 4x4x8 slice. The times are simulated.
256 devices in a mesh: clus: 16 (over y, x), fsdp: 8 (over z), head: 2 (over core).
Axes of the slice: x: 4, y: 4, z: 8, core: 2. Of those that a mesh axis runs over, the one named last changes fastest.
Arguments:
- feats: bfloat16 [32768, 2048], P(('clus', 'fsdp')), as said below
- w_query: float32 [2048, 2048], P(('clus', 'fsdp'), 'head'), may hold values from -0.125 to 0.125
- w_keyval: float32 [2048, 2048], P(('clus', 'fsdp'), 'head'), may hold values from -0.125 to 0.125
- grad_out: bfloat16 [32768, 2048], P(('clus', 'fsdp'), 'head'), may hold values from -6 to 6
- col_block: int32 [256, 5], replicated, may hold values from 0 to 255, as said below
- col_count: int32 [256], replicated, may hold values from 4 to 5
Outputs:
- out: bfloat16 [32768, 2048], P(('clus', 'fsdp'), 'head')
- grad_w_query: float32 [2048, 2048], P(('clus', 'fsdp'), 'head')
- grad_w_keyval: float32 [2048, 2048], P(('clus', 'fsdp'), 'head')
Inputs may be any that keep to these rules, and one draw needn't show every extreme that they name: `col_block`: column 0 of row b is b itself; column 1 is another block of b's cluster (cluster of a block = block // 2); the other columns lie in other clusters whose index differs from b's cluster by a nonzero multiple of 8. A row names each block at most once. The rows of one cluster name, in any other cluster, at most one distinct block. `feats`: node features of order one, rows of differing scale.
All inputs are finite; a program needn't handle non-finite values.
Results may differ from a plain program's by a relative error of at most 0.014.
The roundings to bfloat16 on the way count: a program that leaves them out, or rounds other values in their place, can miss the bound.
Values may be sent and summed in bfloat16 or wider, within the bound.
A program may use at most 128 MiB of HBM per device.

v0:
```python
import math

import jax
import jax.numpy as jnp
from jax import lax
from jax.sharding import PartitionSpec as P

HD = 128
BLK = 128
NCOL = 5


def on_device(feats, w_query, w_keyval, grad_out, col_block, col_count):
    rows = feats.shape[0]
    half = w_query.shape[1]
    nlocal = rows // BLK
    heads_here = half // HD
    nclus = lax.axis_size("clus")
    nfsdp = lax.axis_size("fsdp")
    clus_at = lax.axis_index("clus")
    fsdp_at = lax.axis_index("fsdp")
    myself = clus_at * nfsdp + fsdp_at
    scale = 1.0 / math.sqrt(HD)
    columns = feats
    acc_query = jnp.dot(
        columns,
        lax.all_gather(w_query.astype(jnp.bfloat16), ("clus", "fsdp"), axis=0, tiled=True),
        preferred_element_type=jnp.float32,
    )
    acc_keyval = jnp.dot(
        columns,
        lax.all_gather(w_keyval.astype(jnp.bfloat16), ("clus", "fsdp"), axis=0, tiled=True),
        preferred_element_type=jnp.float32,
    )
    query = acc_query.astype(jnp.bfloat16)
    keyval = acc_keyval.astype(jnp.bfloat16)
    all_cols = col_block.reshape(nclus, nfsdp, nlocal, NCOL)
    all_counts = col_count.reshape(nclus, nfsdp, nlocal)
    peer_cols = lax.dynamic_index_in_dim(all_cols, fsdp_at, 1, keepdims=False)
    peer_counts = lax.dynamic_index_in_dim(all_counts, fsdp_at, 1, keepdims=False)
    peer_live = jnp.arange(NCOL, dtype=jnp.int32)[None, None, :] < peer_counts[:, :, None]
    my_blocks = myself * nlocal + jnp.arange(nlocal, dtype=jnp.int32)
    listed = (peer_cols[:, :, :, None] == my_blocks[None, None, None, :]) & peer_live[:, :, :, None]
    needed = jnp.any(listed, axis=(1, 2)) & (jnp.arange(nclus, dtype=jnp.int32) != clus_at)[:, None]
    flat_keyval = keyval.reshape(nlocal, BLK * half)
    outgoing = jnp.dot(needed.astype(jnp.bfloat16), flat_keyval, preferred_element_type=jnp.float32)
    outgoing = outgoing.astype(jnp.bfloat16).reshape(nclus, BLK, half)
    received = lax.all_to_all(outgoing, "clus", split_axis=0, concat_axis=0, tiled=True)
    my_cols = lax.dynamic_slice_in_dim(col_block, myself * nlocal, nlocal, 0)
    my_counts = lax.dynamic_slice_in_dim(col_count, myself * nlocal, nlocal, 0)
    col_cluster = my_cols // nlocal
    inside = col_cluster == myself
    table_index = jnp.where(inside, my_cols % nlocal, nlocal + col_cluster // nfsdp).reshape(-1)
    table = jnp.concatenate([keyval.reshape(nlocal, BLK, half), received], 0)
    keys = jnp.take(table, table_index, axis=0).reshape(nlocal, NCOL * BLK, heads_here, HD)
    queries = query.reshape(nlocal, BLK, heads_here, HD)
    cotans = grad_out.reshape(nlocal, BLK, heads_here, HD)
    valid = jnp.repeat(jnp.arange(NCOL, dtype=jnp.int32)[None, :] < my_counts[:, None], BLK, axis=1)
    score = jnp.einsum("bqhd,bkhd->bhqk", queries, keys, preferred_element_type=jnp.float32) * scale
    score = jnp.where(valid[:, None, None, :], score, -1e30)
    top = jnp.max(score, axis=-1, keepdims=True)
    expo = jnp.exp(score - top)
    prob = expo / jnp.sum(expo, axis=-1, keepdims=True)
    prob_b = prob.astype(jnp.bfloat16)
    out = (
        jnp.einsum("bhqk,bkhd->bqhd", prob_b, keys, preferred_element_type=jnp.float32)
        .astype(jnp.bfloat16)
        .reshape(rows, half)
    )
    dprob = jnp.einsum("bqhd,bkhd->bhqk", cotans, keys, preferred_element_type=jnp.float32)
    delta = jnp.sum(prob * dprob, axis=-1, keepdims=True)
    dscore = (prob * (dprob - delta)).astype(jnp.bfloat16)
    dquery = (
        (jnp.einsum("bhqk,bkhd->bqhd", dscore, keys, preferred_element_type=jnp.float32) * scale)
        .astype(jnp.bfloat16)
        .reshape(rows, half)
    )
    dkeys = (
        jnp.einsum("bhqk,bqhd->bkhd", dscore, queries, preferred_element_type=jnp.float32) * scale
    )
    dkeys = dkeys + jnp.einsum(
        "bhqk,bqhd->bkhd", prob_b, cotans, preferred_element_type=jnp.float32
    )
    dkeys = dkeys.reshape(nlocal * NCOL, BLK * half)
    onehot = (table_index[:, None] == jnp.arange(nlocal + nclus, dtype=jnp.int32)[None, :]).astype(
        jnp.float32
    )
    grad_table = jnp.dot(onehot.T, dkeys, precision=lax.Precision.HIGHEST)
    returned = lax.all_to_all(
        grad_table[nlocal:].reshape(nclus, BLK, half),
        "clus",
        split_axis=0,
        concat_axis=0,
        tiled=True,
    )
    dkeyval = grad_table[:nlocal] + jnp.dot(
        needed.T.astype(jnp.float32),
        returned.reshape(nclus, BLK * half),
        precision=lax.Precision.HIGHEST,
    )
    dkeyval = dkeyval.astype(jnp.bfloat16).reshape(rows, half)
    both_grads = jnp.concatenate([dquery, dkeyval], 1)
    columns = feats
    partial_sum = lax.psum_scatter(
        lax.dot_general(
            columns, both_grads, (((0,), (0,)), ((), ())), preferred_element_type=jnp.float32
        ).astype(jnp.bfloat16),
        "clus",
        scatter_dimension=0,
        tiled=True,
    ).astype(jnp.float32)
    final = lax.psum_scatter(partial_sum, "fsdp", scatter_dimension=0, tiled=True)
    return (out, final[:, :half], final[:, half:])


def solution(mesh):
    return jax.shard_map(
        on_device,
        mesh=mesh,
        in_specs=(
            P(("clus", "fsdp"), None),
            P(("clus", "fsdp"), "head"),
            P(("clus", "fsdp"), "head"),
            P(("clus", "fsdp"), "head"),
            P(),
            P(),
        ),
        out_specs=(
            P(("clus", "fsdp"), "head"),
            P(("clus", "fsdp"), "head"),
            P(("clus", "fsdp"), "head"),
        ),
        check_vma=False,
    )
```

profile of v0, /device:TPU:1, one launch (start us, length us, event | category | flops | bytes accessed | tf_op | source)
XLA Modules:
  0.0 632.3 jit_solution(5833196491782407962)
XLA Ops:
  12.3 117.0 %all-gather.3.cloned.1.call-done = bf16[2048,1024]{1,0:T(8,128)(2,1)} async-done(((bf16[16,1024]{1,0:T(8,128)(2,1)}), bf16[2048,1024]{1,0:T(8,128)(2,1)}) %all-gather.3.cloned.1.call-update) | async-done | bytes 4194320 | tf_op jit(solution)/shard_map/all_gather | solution.py:32
  129.4 3.4 convolution_convert_fusion.2
  134.8 4.4 copy.107
  139.2 5.3 all-to-all-start
  145.4 128.5 %all-gather.5.cloned.1.call-done = bf16[2048,1024]{1,0:T(8,128)(2,1)} async-done(((bf16[16,1024]{1,0:T(8,128)(2,1)}), bf16[2048,1024]{1,0:T(8,128)(2,1)}) %all-gather.5.cloned.1.call-update) | async-done | bytes 4194320 | tf_op jit(solution)/shard_map/all_gather | solution.py:27
  274.0 3.4 fusion.21
  277.9 4.7 pad_maximum_fusion
  282.7 4.7 gather_fusion
  303.8 6.3 %copy.92 = f32[2,640,8,128]{3,2,1,0:T(8,128)} copy(f32[2,640,8,128]{1,3,2,0:T(8,128)} %bitcast_add_fusion) | data formatting | bytes 10485760 | tf_op jit(solution)/shard_map/add | solution.py:81
  310.1 6.2 reshape.121
  316.3 8.1 %fusion.30 = f32[18,131072]{1,0:T(8,128)S(1)} fusion(f32[10,131072]{1,0:T(8,128)} %reshape.121, s32[10]{0:T(128)S(1)} %reshape.120), kind=kOutput, calls=%fused_computation.50 | convolution fusion | flops 283115712 | bytes 14680104 | tf_op jit(solution)/shard_map/dot_general | solution.py:88
  324.4 4.3 slice.19
  331.5 11.4 %copy.114 = f32[2,8,128,1024]{3,2,1,0:T(8,128)} copy(f32[2,8,128,1024]{3,1,2,0:T(8,128)} %bitcast.85) | data formatting | bytes 16777216
  343.0 5.0 all-to-all-start.1
  348.0 4.8 copy.80
  352.8 3.6 fusion.20
  356.8 105.8 %all-to-all-done.1 = f32[16,128,1024]{2,1,0:T(8,128)} async-done(((f32[16,128,1024]{2,1,0:T(8,128)}), f32[16,128,1024]{2,1,0:T(8,128)}, u32[]{:S(2)}, u32[]{:S(2)}) %all-to-all-start.1) | async-done | bytes 8388640 | tf_op jit(solution)/shard_map/all_to_all | solution.py:89
  462.7 8.2 %copy.115 = f32[2,8,128,1024]{3,1,2,0:T(8,128)S(1)} copy(f32[2,8,128,1024]{3,2,1,0:T(8,128)} %bitcast.38) | data formatting | bytes 16777216
  470.9 5.0 fusion.1
  476.4 5.6 convert_bitcast_fusion
  482.0 12.3 %copy.100 = bf16[2048,2048]{1,0:T(8,128)(2,1)} copy(bf16[2048,2048]{0,1:T(8,128)(2,1)} %convert_bitcast_fusion) | data formatting | bytes 16777216
  494.4 92.4 %reduce-scatter.7.cloned.1.call-done = bf16[128,2048]{1,0:T(8,128)(2,1)} async-done(((bf16[2048,2048]{1,0:T(8,128)(2,1)}), bf16[128,2048]{1,0:T(8,128)(2,1)}) %reduce-scatter.7.cloned.1.call-update) | async-done | bytes 524304
  589.4 4.4 fusion.22
  595.0 28.9 %reduce-scatter.9.cloned.1.call-done = f32[16,2048]{1,0:T(8,128)} async-done(((f32[128,2048]{1,0:T(8,128)}), f32[16,2048]{1,0:T(8,128)}) %reduce-scatter.9.cloned.1.call-update) | async-done | bytes 131088
  (71 shorter events, 33.9 us)
Async XLA Ops:
  7.2 122.2 %copy-start = (bf16[256,2048]{1,0:T(8,128)(2,1)S(1)}, bf16[256,2048]{1,0:T(8,128)(2,1)}, u32[]{:S(2)}) copy-start(bf16[256,2048]{1,0:T(8,128)(2,1)} %param.6) | copy-start | bytes 3145732
  7.2 122.2 %all-gather.3.cloned.1.call-start = ((), (), s32[]{:S(2)}) async-start(), calls=%async_computation.4 | async-start | bytes 4227072 | tf_op jit(solution)/shard_map/all_gather | solution.py:32
  8.8 265.2 %all-gather.5.cloned.1.call-start = ((), (), s32[]{:S(2)}) async-start(), calls=%async_computation.5 | async-start | bytes 4227072 | tf_op jit(solution)/shard_map/all_gather | solution.py:27
  139.2 5.3 copy-start.7
  139.2 5.4 copy-start.6
  139.2 6.1 copy-start.5
  139.2 138.7 %all-to-all-start = ((bf16[16,128,1024]{2,1,0:T(8,128)(2,1)}), bf16[16,128,1024]{2,1,0:T(8,128)(2,1)}, u32[]{:S(2)}, u32[]{:S(2)}) async-start(bf16[16,128,1024]{2,1,0:T(8,128)(2,1)} %bitcast.87), calls=%async_computation | async-start | bytes 8388608 | tf_op jit(solution)/shard_map/all_to_all | solution.py:48
  292.4 3.0 copy-start.2
  295.4 5.4 copy-start.4
  298.4 1.5 copy-start.3
  324.4 7.1 %copy-start.1 = (f32[18,131072]{1,0:T(8,128)}, f32[18,131072]{1,0:T(8,128)S(1)}, u32[]{:S(2)}) copy-start(f32[18,131072]{1,0:T(8,128)S(1)} %fusion.30) | copy-start | bytes 28311556
  343.0 119.7 %all-to-all-start.1 = ((f32[16,128,1024]{2,1,0:T(8,128)}), f32[16,128,1024]{2,1,0:T(8,128)}, u32[]{:S(2)}, u32[]{:S(2)}) async-start(f32[16,128,1024]{2,1,0:T(8,128)} %bitcast.83), calls=%async_computation.1 | async-start | bytes 16777216 | tf_op jit(solution)/shard_map/all_to_all | solution.py:89
  347.9 238.8 %reduce-scatter.7.cloned.1.call-start = ((), (), s32[]{:S(2)}) async-start(), calls=%async_computation.6 | async-start | bytes 8912896
  494.4 129.5 %reduce-scatter.9.cloned.1.call-start = ((), (), s32[]{:S(2)}) async-start(), calls=%async_computation.7 | async-start | bytes 1179648
Sparse Core Ops, SparseCore 0:
  12.2 117.0 all-gather.2
  133.5 140.3 all-gather.4
  494.5 92.2 reduce-scatter.6
  589.5 34.3 reduce-scatter.8
where the time goes:
time: 642 us; the launch traced here: 632 us
  waiting for transfers between devices  473 us (74%)
  local copies, waits for them, and re-layouts  78.9 us (12%)
  matrix products  42.3 us (7%)
  between operations  14.5 us (2%)
  other arithmetic  13.5 us (2%)
  starting transfers between devices  10.4 us (2%)
    all_gather x1, waiting for transfers between devices, on_device(): lax.all_gather(w_query.astype(jnp.bfloat16), ('clus', 'fsdp'), axis=0, ti...  129 us
    unnamed x6, waiting for transfers between devices  121 us
    all_gather x1, waiting for transfers between devices, on_device(): lax.all_gather(w_keyval.astype(jnp.bfloat16), ('clus', 'fsdp'), axis=0, t...  117 us
    all_to_all x1, waiting for transfers between devices, on_device(): lax.all_to_all(grad_table[nlocal:].reshape(nclus, BLK, half), 'clus', spl...  106 us
    unnamed x32, local copies, waits for them, and re-layouts  47.8 us
  transfers between devices with their start and end apart: 6, of which 5 were waited for; matrix products, arithmetic and copies ran while one was open for 5% of the time, Pallas kernels for 0%

commit v1 on v0

v1 whole, which is shorter than its diff:
```python
import functools
import math

import jax
import jax.numpy as jnp
from jax import lax
from jax.experimental import pallas as pl
from jax.experimental.pallas import tpu as pltpu
from jax.sharding import PartitionSpec as P

D = 2048
HD = 128
BLK = 128
NCOL = 5
SIDE = 4
NC = 16
NZ = 8
HALF = 1024
PER = 8
WROWS = 16
SCALE = 1.0 / math.sqrt(HD)
BF = jnp.bfloat16
F32 = jnp.float32
NT = (((1,), (1,)), ((), ()))
NN = (((1,), (0,)), ((), ()))


def here():
    return lax.axis_index("clus"), lax.axis_index("fsdp"), lax.axis_index("head")


def remote(src, dst, send, recv, device):
    return pltpu.make_async_remote_copy(
        src_ref=src,
        dst_ref=dst,
        send_sem=send,
        recv_sem=recv,
        device_id=device,
        device_id_type=pl.DeviceIdType.MESH,
    )


def greet_all(clus, fsdp, core):
    barrier = pltpu.get_barrier_semaphore()

    @pl.loop(0, 2 * NC)
    def _(i):
        other, side = i // 2, i % 2

        @pl.when(jnp.logical_or(other != clus, side != core))
        def _():
            pl.semaphore_signal(
                barrier, inc=1, device_id=(other, fsdp, side), device_id_type=pl.DeviceIdType.MESH
            )

    @pl.loop(1, NZ)
    def _(i):
        pl.semaphore_signal(
            barrier,
            inc=1,
            device_id=(clus, (fsdp + i) % NZ, core),
            device_id_type=pl.DeviceIdType.MESH,
        )

    pl.semaphore_wait(barrier, 2 * NC - 1 + NZ - 1)


def gather_kernel(
    feats,
    w_query,
    w_keyval,
    grad_out,
    feats_out,
    q_out,
    kv_out,
    cot_out,
    rows,
    wb,
    wall,
    ring_send,
    ring_recv,
    local_sem,
    save_sem,
    col_send,
    col_recv,
    z_send,
    z_recv,
    swap_send,
    swap_recv,
    cot_send,
    cot_recv,
    kv_send,
    kv_recv,
):
    clus, fsdp, core = here()
    xp, yp = clus % SIDE, clus // SIDE

    def at(dx, dy):
        return ((yp + dy) % SIDE) * SIDE + (xp + dx) % SIDE

    wb[0] = w_query[...].astype(BF)
    wb[1] = w_keyval[...].astype(BF)
    greet_all(clus, fsdp, core)

    def slot(half, first, second):
        return at(first, second) if half == 0 else at(second, first)

    def hop(half, axis, step):
        return slot(half, step, 0) if axis == 0 else slot(half, 0, step)

    def ring(half, label, src, part, own):
        index = half * 20 + label
        axis = 0 if label < 4 else 1
        step = 1 if label % 2 == 0 else -1
        start = half * 64 + (32 if part == 2 else 0)
        count = 64 if part == 0 else 32
        if own:
            source = feats.at[pl.ds(pl.multiple_of(core * BLK, BLK) + start, count)]
        else:
            source = rows.at[src, pl.ds(start, count)]
        return remote(
            source,
            rows.at[src, pl.ds(start, count)],
            ring_send.at[index],
            ring_recv.at[index],
            (hop(half, axis, step), fsdp, core),
        )

    OFF = (0, -1, 1, 2)
    plan = {}
    for half in (0, 1):
        plan[half, 0] = (slot(half, 0, 0), slot(half, -1, 0), 0)
        plan[half, 1] = (slot(half, 0, 0), slot(half, 1, 0), 0)
        plan[half, 2] = (slot(half, -1, 0), slot(half, -2, 0), 1)
        plan[half, 3] = (slot(half, 1, 0), slot(half, 2, 0), 2)
        for k, o in enumerate(OFF):
            base = 4 + 4 * k
            plan[half, base] = (slot(half, o, 0), slot(half, o, -1), 0)
            plan[half, base + 1] = (slot(half, o, 0), slot(half, o, 1), 0)
            plan[half, base + 2] = (slot(half, o, -1), slot(half, o, -2), 1)
            plan[half, base + 3] = (slot(half, o, 1), slot(half, o, 2), 2)

    def send(*labels):
        for label in labels:
            for half in (0, 1):
                src, _, part = plan[half, label]
                ring(half, label, src, part, label in (0, 1, 4, 5)).start()

    def arrived(*labels):
        for label in labels:
            for half in (0, 1):
                _, dst, part = plan[half, label]
                ring(half, label, dst, part, False).wait_recv()

    send(0, 1)

    def column_copy(j, part):
        head = core * PER + j
        src = wb.at[part, :, pl.ds(pl.multiple_of(j * HD, HD), HD)]
        dst = wall.at[part, clus, fsdp]
        return head, src, dst

    @pl.loop(0, PER)
    def _(i):
        j = (i + clus) % PER
        for part in (0, 1):
            head, src, dst = column_copy(j, part)
            mine = jnp.logical_and(head == clus, core == part)

            @pl.when(mine)
            def _():
                pltpu.make_async_copy(src, dst, col_recv.at[clus]).start()

            @pl.when(jnp.logical_not(mine))
            def _():
                remote(
                    src, dst, col_send.at[2 * j + part], col_recv.at[clus], (head, fsdp, part)
                ).start()

    own_rows = pltpu.make_async_copy(
        feats.at[pl.ds(pl.multiple_of(core * BLK, BLK), BLK)], rows.at[clus], local_sem
    )
    own_rows.start()
    send(4, 5)

    @pl.loop(0, NC)
    def _(i):
        remote(
            wb.at[0, :, pl.ds(0, HD)],
            wall.at[core, i, fsdp],
            col_send.at[0],
            col_recv.at[i],
            (clus, fsdp, 1 - core),
        ).wait_recv()

    def z_copy(i):
        other = (fsdp + i) % NZ
        return remote(
            wall.at[core, :, fsdp],
            wall.at[core, :, fsdp],
            z_send.at[i],
            z_recv.at[i],
            (clus, other, core),
        )

    @pl.loop(1, NZ)
    def _(i):
        z_copy(i).start()

    def cot_copy(j, block):
        head = core * PER + j
        src = grad_out.at[
            pl.ds(block * BLK, BLK), pl.ds(pl.multiple_of(j * HD, HD), HD)
        ]
        return head, src, cot_out.at[clus]

    @pl.loop(0, PER)
    def _(i):
        j = (i + clus) % PER
        for block in (0, 1):
            head, src, dst = cot_copy(j, block)
            mine = jnp.logical_and(head == clus, core == block)

            @pl.when(mine)
            def _():
                pltpu.make_async_copy(src, dst, cot_recv.at[clus]).start()

            @pl.when(jnp.logical_not(mine))
            def _():
                remote(
                    src, dst, cot_send.at[2 * j + block], cot_recv.at[clus], (head, fsdp, block)
                ).start()

    arrived(0, 1)
    send(2, 3, 8, 9, 12, 13)

    @pl.loop(1, NZ)
    def _(i):
        other = (fsdp + NZ - i) % NZ
        remote(
            wall.at[core, :, other],
            wall.at[core, :, other],
            z_send.at[i],
            z_recv.at[i],
            (clus, other, core),
        ).wait_recv()

    swap = remote(
        wall.at[core], wall.at[core], swap_send, swap_recv, (clus, fsdp, 1 - core)
    )
    swap.start()
    arrived(4, 5)
    send(6, 7)
    arrived(2, 3)
    send(16, 17)
    remote(
        wall.at[1 - core], wall.at[1 - core], swap_send, swap_recv, (clus, fsdp, 1 - core)
    ).wait_recv()
    own_rows.wait()

    saved = []
    shared = []

    def project(dx, dy):
        src = at(dx, dy)
        index = len(saved)
        save = pltpu.make_async_copy(rows.at[src], feats_out.at[src], save_sem.at[index])
        save.start()
        weights = jnp.concatenate(
            [wall[0].reshape(D, HD), wall[1].reshape(D, HD)], axis=1
        )
        both = lax.dot_general(rows[src], weights, NN, preferred_element_type=F32)
        q_out[src] = both[:, :HD].astype(BF)
        keys = both[:, HD:]
        mine = 2 * src + core
        kv_out[mine, 0] = keys.astype(BF)
        kv_out[mine, 1] = keys.T.astype(BF)
        share = remote(
            kv_out.at[mine],
            kv_out.at[mine],
            kv_send.at[index],
            kv_recv.at[index],
            (clus, fsdp, 1 - core),
        )
        share.start()
        theirs = 2 * src + 1 - core
        saved.append(save)
        shared.append(
            (
                share,
                remote(
                    kv_out.at[theirs],
                    kv_out.at[theirs],
                    kv_send.at[index],
                    kv_recv.at[index],
                    (clus, fsdp, 1 - core),
                ),
            )
        )

    project(0, 0)
    arrived(8, 9, 12, 13)
    send(10, 11, 14, 15)
    project(1, 0)
    project(-1, 0)
    project(0, 1)
    arrived(16, 17)
    send(18, 19)
    project(0, -1)
    project(1, 1)
    project(-1, 1)
    project(1, -1)
    project(-1, -1)
    arrived(6, 7)
    project(2, 0)
    project(0, 2)
    arrived(10, 11, 14, 15)
    project(2, 1)
    project(2, -1)
    project(1, 2)
    project(-1, 2)
    arrived(18, 19)
    project(2, 2)

    @pl.loop(0, NC)
    def _(i):
        remote(
            grad_out.at[pl.ds(0, BLK), pl.ds(0, HD)],
            cot_out.at[i],
            cot_send.at[0],
            cot_recv.at[i],
            (clus, fsdp, 1 - core),
        ).wait_recv()

    @pl.loop(0, PER)
    def _(j):
        for part in (0, 1):
            head, src, dst = column_copy(j, part)
            _, csrc, cdst = cot_copy(j, part)

            @pl.when(jnp.logical_not(jnp.logical_and(head == clus, core == part)))
            def _():
                remote(
                    src, dst, col_send.at[2 * j + part], col_recv.at[clus], (head, fsdp, part)
                ).wait_send()
                remote(
                    csrc, cdst, cot_send.at[2 * j + part], cot_recv.at[clus], (head, fsdp, part)
                ).wait_send()

    @pl.loop(1, NZ)
    def _(i):
        z_copy(i).wait_send()

    swap.wait_send()
    for label in range(20):
        for half in (0, 1):
            src, _, part = plan[half, label]
            ring(half, label, src, part, label in (0, 1, 4, 5)).wait_send()
    for save, (share, theirs) in zip(saved, shared):
        save.wait()
        share.wait_send()
        theirs.wait_recv()


def attend_kernel(q, kv, cot, col_block, col_count, out, dqt, own, sib, total):
    clus, fsdp, core = here()
    total[...] = jnp.zeros_like(total)

    def step(i, carry):
        block = 2 * NZ * i + 2 * fsdp + core
        cols = [col_block[block, k] for k in range(NCOL)]
        cols = [(c // (2 * NZ)) * 2 + c % 2 for c in cols]
        count = col_count[block]
        query, grad = q[i], cot[i]
        keys = jnp.concatenate([kv[c, 0] for c in cols], axis=0)
        keys_t = jnp.concatenate([kv[c, 1] for c in cols], axis=1)
        both = lax.dot_general(
            keys, jnp.concatenate([query, grad], axis=0), NT, preferred_element_type=F32
        )
        score = both[:, :BLK] * SCALE
        dprob = both[:, BLK:]
        place = lax.broadcasted_iota(jnp.int32, score.shape, 0) // BLK
        score = jnp.where(place < count, score, -1e30)
        top = jnp.max(score, axis=0, keepdims=True)
        expo = jnp.exp(score - top)
        prob = expo * (1.0 / jnp.sum(expo, axis=0, keepdims=True))
        delta = jnp.sum(prob * dprob, axis=0, keepdims=True)
        dscore = (prob * (dprob - delta)).astype(BF)
        prob_b = prob.astype(BF)
        both_t = lax.dot_general(
            keys_t,
            jnp.concatenate([dscore, prob_b], axis=1),
            NN,
            preferred_element_type=F32,
        )
        dqt[:, pl.ds(pl.multiple_of(i * BLK, BLK), BLK)] = (both_t[:, :BLK] * SCALE).astype(BF)
        out[i] = both_t[:, BLK:].T.astype(BF)
        dkeys = (
            lax.dot_general(dscore, query, NN, preferred_element_type=F32) * SCALE
            + lax.dot_general(prob_b, grad, NN, preferred_element_type=F32)
        )
        for k, c in enumerate(cols):
            total[c // 2, c % 2] += dkeys[k * BLK : (k + 1) * BLK]
        return carry

    lax.fori_loop(0, NC, step, 0, unroll=2)
    own[...] = total[:, core]
    sib[...] = total[:, 1 - core].astype(BF)


def scatter_kernel(
    feats,
    out_blocks,
    dqt,
    own,
    sib,
    out,
    grad_q,
    grad_k,
    rows,
    other,
    dkt,
    part_send,
    part_recv,
    part_own,
    z_out,
    z_in,
    fin,
    load_sem,
    dk_sem,
    out_send,
    out_recv,
    half_send,
    half_recv,
    z_send,
    z_recv,
    fin_send,
    fin_recv,
):
    clus, fsdp, core = here()
    CH = 256
    NCH = D // CH
    greet_all(clus, fsdp, core)
    give = remote(sib, other, dk_sem.at[0], dk_sem.at[1], (clus, fsdp, 1 - core))
    give.start()

    def chunk(n):
        return (n + (1 - core) * (NCH // 2)) % NCH

    def load(n):
        cols = pl.ds(pl.multiple_of(chunk(n) * CH, CH), CH)
        return pltpu.make_async_copy(
            feats.at[:, :, cols], rows.at[:, :, cols], load_sem.at[n]
        )

    for n in range(NCH):
        load(n).start()

    def out_copy(s):
        return remote(
            out_blocks.at[s],
            out.at[
                pl.ds(pl.multiple_of(core * BLK, BLK), BLK),
                pl.ds(pl.multiple_of((clus % PER) * HD, HD), HD),
            ],
            out_send.at[s],
            out_recv.at[2 * (clus % PER) + core],
            (s, fsdp, clus // PER),
        )

    own_out = core == clus // PER

    @pl.loop(0, NC)
    def _(i):
        s = (i + clus) % NC
        mine = jnp.logical_and(s == clus, own_out)

        @pl.when(mine)
        def _():
            pltpu.make_async_copy(
                out_blocks.at[s],
                out.at[
                    pl.ds(pl.multiple_of(core * BLK, BLK), BLK),
                    pl.ds(pl.multiple_of((clus % PER) * HD, HD), HD),
                ],
                out_recv.at[2 * (clus % PER) + core],
            ).start()

        @pl.when(jnp.logical_not(mine))
        def _():
            out_copy(s).start()

    def half_copy(t):
        return remote(
            part_send.at[t],
            part_recv.at[t],
            half_send.at[t],
            half_recv.at[t],
            (clus, fsdp, 1 - core),
        )

    def z_copy(t, i):
        to = (fsdp + i) % NZ
        return remote(
            z_out.at[t, to],
            z_in.at[t, fsdp],
            z_send.at[t, i],
            z_recv.at[t, i],
            (clus, to, core),
        )

    def gradient(t, lhs):
        for n in range(NCH):
            if t == 0:
                load(n).wait()
            cols = pl.ds(pl.multiple_of(chunk(n) * CH, CH), CH)
            part = lax.dot_general(
                lhs[...],
                rows[:, :, cols].reshape(NC * BLK, CH),
                NN,
                preferred_element_type=F32,
            )
            for k in range(CH // BLK):
                piece = part[:, k * BLK : (k + 1) * BLK].T.reshape(NZ, WROWS, HD)
                index = (n * CH) // BLK + k
                if index < PER:
                    part_send[t, index] = piece.astype(BF)
                else:
                    part_own[t, index - PER] = piece
            if n == NCH // 2 - 1:
                half_copy(t).start()
        half_copy(t).wait_recv()
        for k in range(PER):
            total = part_own[t, k] + part_recv[t, k].astype(F32)
            part_own[t, k] = total
            z_out[t, :, k] = total.astype(BF)

        @pl.loop(1, NZ)
        def _(i):
            z_copy(t, i).start()

    gradient(0, dqt)
    give.wait_recv()
    for s in range(NC):
        total = own[s] + other[s].astype(F32)
        dkt[:, s * BLK : (s + 1) * BLK] = total.astype(BF).astype(F32).T.astype(BF)
    gradient(1, dkt)

    def fin_copy(t, k):
        dest = (grad_q, grad_k)[t]
        to = core * PER + k
        return (
            to,
            fin.at[t, k],
            dest.at[:, pl.ds(pl.multiple_of((clus % PER) * HD, HD), HD)],
            fin_recv.at[t, clus % PER],
        )

    for t in (0, 1):
        for i in range(1, NZ):
            frm = (fsdp + NZ - i) % NZ
            remote(
                z_out.at[t, 0],
                z_in.at[t, frm],
                z_send.at[t, i],
                z_recv.at[t, i],
                (clus, frm, core),
            ).wait_recv()
        for k in range(PER):
            total = part_own[t, k, fsdp]
            for i in range(1, NZ):
                total += z_in[t, (fsdp + NZ - i) % NZ, k].astype(F32)
            fin[t, k] = total
        for k in range(PER):
            to, src, dst, recv = fin_copy(t, k)

            @pl.when(to == clus)
            def _():
                pltpu.make_async_copy(src, dst, recv).start()

            @pl.when(to != clus)
            def _():
                remote(src, dst, fin_send.at[t, k], recv, (to, fsdp, clus // PER)).start()

    give.wait_send()
    for t in (0, 1):
        half_copy(t).wait_send()

        @pl.loop(1, NZ)
        def _(i):
            z_copy(t, i).wait_send()

        for k in range(PER):
            to, src, dst, recv = fin_copy(t, k)

            @pl.when(to != clus)
            def _():
                remote(src, dst, fin_send.at[t, k], recv, (to, fsdp, clus // PER)).wait_send()

    @pl.loop(0, NC)
    def _(s):
        @pl.when(jnp.logical_not(jnp.logical_and(s == clus, own_out)))
        def _():
            out_copy(s).wait_send()

    for m in range(PER):
        for block in (0, 1):
            remote(
                out_blocks.at[0],
                out.at[pl.ds(block * BLK, BLK), pl.ds(m * HD, HD)],
                out_send.at[0],
                out_recv.at[2 * m + block],
                (clus, fsdp, 1 - core),
            ).wait_recv()
        for t in (0, 1):
            remote(
                fin.at[t, 0],
                (grad_q, grad_k)[t].at[:, pl.ds(m * HD, HD)],
                fin_send.at[t, 0],
                fin_recv.at[t, m],
                (clus, fsdp, 1 - core),
            ).wait_recv()


ANY = pl.BlockSpec(memory_space=pl.ANY)
VM = pl.BlockSpec(memory_space=pltpu.VMEM)
SM = pl.BlockSpec(memory_space=pltpu.SMEM)
DMA = pltpu.SemaphoreType.DMA
LIMIT = 56 * 1024 * 1024


def shape(dims, kind):
    return jax.ShapeDtypeStruct(dims, kind)


def on_device(feats, w_query, w_keyval, grad_out, col_block, col_count):
    feats_all, query, keyval, cots = pl.pallas_call(
        gather_kernel,
        name="gather_project",
        out_shape=(
            shape((NC, BLK, D), BF),
            shape((NC, BLK, HD), BF),
            shape((2 * NC, 2, BLK, HD), BF),
            shape((NC, BLK, HD), BF),
        ),
        in_specs=[ANY, VM, VM, ANY],
        out_specs=(ANY, VM, VM, VM),
        scratch_shapes=[
            pltpu.VMEM((NC, BLK, D), BF),
            pltpu.VMEM((2, WROWS, HALF), BF),
            pltpu.VMEM((2, NC, NZ, WROWS, HD), BF),
            DMA((40,)),
            DMA((40,)),
            DMA,
            DMA((NC,)),
            DMA((16,)),
            DMA((NC,)),
            DMA((NZ,)),
            DMA((NZ,)),
            DMA,
            DMA,
            DMA((16,)),
            DMA((NC,)),
            DMA((NC,)),
            DMA((NC,)),
        ],
        compiler_params=pltpu.CompilerParams(
            collective_id=1, has_side_effects=True, vmem_limit_bytes=LIMIT
        ),
        cost_estimate=pl.CostEstimate(
            flops=2 * D * D * 256, bytes_accessed=18 << 20, transcendentals=0
        ),
    )(feats, w_query, w_keyval, grad_out)
    out_blocks, dqt, own, sib = pl.pallas_call(
        attend_kernel,
        name="attend",
        out_shape=(
            shape((NC, BLK, HD), BF),
            shape((HD, NC * BLK), BF),
            shape((NC, BLK, HD), F32),
            shape((NC, BLK, HD), BF),
        ),
        in_specs=[VM, VM, VM, SM, SM],
        out_specs=(VM, VM, VM, VM),
        scratch_shapes=[pltpu.VMEM((NC, 2, BLK, HD), F32)],
        compiler_params=pltpu.CompilerParams(vmem_limit_bytes=LIMIT),
        cost_estimate=pl.CostEstimate(
            flops=12 * NC * BLK * 640 * HD, bytes_accessed=6 << 20, transcendentals=NC * BLK * 640
        ),
    )(query, keyval, cots, col_block, col_count)
    return pl.pallas_call(
        scatter_kernel,
        name="scatter_grads",
        out_shape=(
            shape((2 * BLK, HALF), BF),
            shape((WROWS, HALF), F32),
            shape((WROWS, HALF), F32),
        ),
        in_specs=[ANY, VM, VM, VM, VM],
        out_specs=(VM, VM, VM),
        scratch_shapes=[
            pltpu.VMEM((NC, BLK, D), BF),
            pltpu.VMEM((NC, BLK, HD), BF),
            pltpu.VMEM((HD, NC * BLK), BF),
            pltpu.VMEM((2, PER, NZ, WROWS, HD), BF),
            pltpu.VMEM((2, PER, NZ, WROWS, HD), BF),
            pltpu.VMEM((2, PER, NZ, WROWS, HD), F32),
            pltpu.VMEM((2, NZ, PER, WROWS, HD), BF),
            pltpu.VMEM((2, NZ, PER, WROWS, HD), BF),
            pltpu.VMEM((2, PER, WROWS, HD), F32),
            DMA((8,)),
            DMA((2,)),
            DMA((NC,)),
            DMA((NC,)),
            DMA((2,)),
            DMA((2,)),
            DMA((2, NZ)),
            DMA((2, NZ)),
            DMA((2, PER)),
            DMA((2, PER)),
        ],
        compiler_params=pltpu.CompilerParams(
            collective_id=2, has_side_effects=True, vmem_limit_bytes=LIMIT
        ),
        cost_estimate=pl.CostEstimate(
            flops=2 * D * D * 256, bytes_accessed=12 << 20, transcendentals=0
        ),
    )(feats_all, out_blocks, dqt, own, sib)


def solution(mesh):
    return jax.shard_map(
        on_device,
        mesh=mesh,
        in_specs=(
            P(("clus", "fsdp"), None),
            P(("clus", "fsdp"), "head"),
            P(("clus", "fsdp"), "head"),
            P(("clus", "fsdp"), "head"),
            P(),
            P(),
        ),
        out_specs=(
            P(("clus", "fsdp"), "head"),
            P(("clus", "fsdp"), "head"),
            P(("clus", "fsdp"), "head"),
        ),
        check_vma=False,
    )
```

time: 642 us -> 124 us (0.19); the launches traced: 632 us -> 123 us
  waiting for transfers between devices: 473 us -> 0 us
  Pallas kernels: 0 us -> 117 us
  local copies, waits for them, and re-layouts: 78.9 us -> 6.3 us
  matrix products: 42.3 us -> 0 us
  between operations: 14.5 us -> 0.65 us
  other arithmetic: 13.5 us -> 0 us
  starting transfers between devices: 10.4 us -> 0 us
    all_gather x2 -> x0, waiting for transfers between devices: 246 us -> none  [the longest x1 129 us: on_device(): lax.all_gather(w_query.astype(jnp.bfloat16), ('clus', 'fsdp'), axis=0, ti...]
    unnamed x6 -> x0, waiting for transfers between devices: 121 us -> none
    pallas_call x0 -> x3, Pallas kernels: none -> 117 us  [the longest x1 67.6 us: on_device(): pl.pallas_call(gather_kernel, name='gather_project', out_shape=(shape((NC...]
    all_to_all x2 -> x0, waiting for transfers between devices: 106 us -> none  [the longest x1 106 us: on_device(): lax.all_to_all(grad_table[nlocal:].reshape(nclus, BLK, half), 'clus', spl...]
    dot_general x12 -> x0, matrix products: 42.3 us -> none  [the longest x1 8.1 us: on_device(): grad_table = jnp.dot(onehot.T, dkeys, precision=lax.Precision.HIGHEST)]
    unnamed x32 -> x4, local copies, waits for them, and re-layouts: 47.8 us -> 6.3 us
    all_to_all x2 -> x0, starting transfers between devices: 10.3 us -> none  [the longest x1 5.3 us: on_device(): lax.all_to_all(outgoing, 'clus', split_axis=0, concat_axis=0, tiled=True)]
    reshape x7 -> x0, local copies, waits for them, and re-layouts: 8.37 us -> none  [the longest x1 6.16 us: on_device(): dkeys = dkeys.reshape(nlocal * NCOL, BLK * half)]
  transfers between devices with their start and end apart: 6 -> 0, of which waited for: 5 -> 0; matrix products, arithmetic and copies ran while one was open for 5% -> 0% of each run, Pallas kernels for 0% -> 0%
where the time goes in v1:
time: 124 us; the launch traced here: 123 us
  Pallas kernels  117 us (94%)
  local copies, waits for them, and re-layouts  6.3 us (5%)
    pallas_call x1, Pallas kernels, on_device(): pl.pallas_call(gather_kernel, name='gather_project', out_shape=(shape((NC...  67.6 us
    pallas_call x1, Pallas kernels, on_device(): pl.pallas_call(scatter_kernel, name='scatter_grads', out_shape=(shape((2...  31.3 us
    pallas_call x1, Pallas kernels, on_device(): pl.pallas_call(attend_kernel, name='attend', out_shape=(shape((NC, BLK, H...  17.7 us
    unnamed x4, local copies, waits for them, and re-layouts  6.3 us

profile of v1, /device:TPU:1, one launch (start us, length us, event | category | flops | bytes accessed | tf_op | source)
XLA Modules:
  0.0 123.5 jit_solution(14342442877058731432)
XLA Ops:
  0.6 1.5 %copy.9.col_block = s32[256,5]{1,0:T(8,128)} copy(s32[256,5]{0,1:T(8,128)} %param.10) | data formatting | bytes 10240 | tf_op args[4]
  2.1 67.6 %gather_project.1 = (bf16[16,128,2048]{2,1,0:T(8,128)(2,1)}, bf16[16,128,128]{2,1,0:T(8,128)(2,1)}, bf16[32,2,128,128]{3,2,1,0:T(8,128)(2,1)}, bf16[16,128,128]{2,1,0:T(8,128)(2,1)}) custom-call(bf16[256,2048]{1,0:T(8,128)(2,1)} %feats.1, f32[16,1024]{1,0:T(8,128)} %w_query.1, f32[16,1024]{1,0:T(8,128)} %w_keyval.1, bf16[256,1024]{1,0:T(8,128)(2,1)} %grad_out.1), custom_call_target="tpu_custom_call" | custom-call | flops 2147483648 | bytes 18874368 | tf_op jit(solution)/shard_map/gather_project/pallas_call | solution.py:637
  69.7 17.7 %attend.1 = (bf16[16,128,128]{2,1,0:T(8,128)(2,1)}, bf16[128,2048]{1,0:T(8,128)(2,1)}, f32[16,128,128]{2,1,0:T(8,128)}, bf16[16,128,128]{2,1,0:T(8,128)(2,1)}) custom-call(bf16[16,128,128]{2,1,0:T(8,128)(2,1)} %get-tuple-element.12.q, bf16[32,2,128,128]{3,2,1,0:T(8,128)(2,1)} %get-tuple-element.13.kv, bf16[16,128,128]{2,1,0:T(8,128)(2,1)} %get-tuple-element.14.cot, ...), custom_call_target="tpu_custom_call" | custom-call | flops 2013265920 | bytes 6291456 | tf_op jit(solution)/shard_map/attend/pallas_call | solution.py:674
  87.4 31.3 %scatter_grads.1 = (bf16[256,1024]{1,0:T(8,128)(2,1)}, f32[16,1024]{1,0:T(8,128)}, f32[16,1024]{1,0:T(8,128)}) custom-call(bf16[16,128,2048]{2,1,0:T(8,128)(2,1)} %get-tuple-element.11.feats, bf16[16,128,128]{2,1,0:T(8,128)(2,1)} %get-tuple-element.15.out_blocks, bf16[128,2048]{1,0:T(8,128)(2,1)} %get-tuple-element.16.dqt, ...), custom_call_target="tpu_custom_call" | custom-call | flops 2147483648 | bytes 12582912 | tf_op jit(solution)/shard_map/scatter_grads/pallas_call | solution.py:691
  118.7 1.9 %copy.13 = bf16[256,1024]{1,0:T(8,128)(2,1)} copy(bf16[256,1024]{1,0:T(8,128)(2,1)} %get-tuple-element.22) | data formatting | bytes 1048576
  120.5 1.5 %copy.14 = f32[16,1024]{1,0:T(8,128)} copy(f32[16,1024]{1,0:T(8,128)} %get-tuple-element.23) | data formatting | bytes 131072
  122.0 1.5 %copy.15 = f32[16,1024]{1,0:T(8,128)} copy(f32[16,1024]{1,0:T(8,128)} %get-tuple-element.24) | data formatting | bytes 131072

commit v2 on v1

--- a/solution.py
+++ b/solution.py
@@ -19,6 +19,7 @@
 PER = 8
 WROWS = 16
 SCALE = 1.0 / math.sqrt(HD)
+LOG2 = SCALE / math.log(2.0)
 BF = jnp.bfloat16
 F32 = jnp.float32
 NT = (((1,), (1,)), ((), ()))
@@ -40,18 +41,18 @@
     )
 
 
-def greet_all(clus, fsdp, core):
+def greet(clus, fsdp, core):
     barrier = pltpu.get_barrier_semaphore()
 
-    @pl.loop(0, 2 * NC)
-    def _(i):
-        other, side = i // 2, i % 2
-
-        @pl.when(jnp.logical_or(other != clus, side != core))
-        def _():
-            pl.semaphore_signal(
-                barrier, inc=1, device_id=(other, fsdp, side), device_id_type=pl.DeviceIdType.MESH
-            )
+    @pl.loop(0, NC)
+    def _(i):
+        for side in (0, 1):
+
+            @pl.when(jnp.logical_or(i != clus, side != core))
+            def _():
+                pl.semaphore_signal(
+                    barrier, inc=1, device_id=(i, fsdp, side), device_id_type=pl.DeviceIdType.MESH
+                )
 
     @pl.loop(1, NZ)
     def _(i):
@@ -62,7 +63,9 @@
             device_id_type=pl.DeviceIdType.MESH,
         )
 
-    pl.semaphore_wait(barrier, 2 * NC - 1 + NZ - 1)
+
+def greeted():
+    pl.semaphore_wait(pltpu.get_barrier_semaphore(), 2 * NC - 1 + NZ - 1)
 
 
 def gather_kernel(
@@ -70,17 +73,15 @@
     w_query,
     w_keyval,
     grad_out,
-    feats_out,
+    rows,
     q_out,
     kv_out,
     cot_out,
-    rows,
     wb,
     wall,
     ring_send,
     ring_recv,
     local_sem,
-    save_sem,
     col_send,
     col_recv,
     z_send,
@@ -98,9 +99,10 @@
     def at(dx, dy):
         return ((yp + dy) % SIDE) * SIDE + (xp + dx) % SIDE
 
+    greet(clus, fsdp, core)
     wb[0] = w_query[...].astype(BF)
     wb[1] = w_keyval[...].astype(BF)
-    greet_all(clus, fsdp, core)
+    greeted()
 
     def slot(half, first, second):
         return at(first, second) if half == 0 else at(second, first)
@@ -258,14 +260,11 @@
     ).wait_recv()
     own_rows.wait()
 
-    saved = []
     shared = []
 
     def project(dx, dy):
         src = at(dx, dy)
-        index = len(saved)
-        save = pltpu.make_async_copy(rows.at[src], feats_out.at[src], save_sem.at[index])
-        save.start()
+        index = len(shared)
         weights = jnp.concatenate(
             [wall[0].reshape(D, HD), wall[1].reshape(D, HD)], axis=1
         )
@@ -284,7 +283,6 @@
         )
         share.start()
         theirs = 2 * src + 1 - core
-        saved.append(save)
         shared.append(
             (
                 share,
@@ -356,68 +354,76 @@
         for half in (0, 1):
             src, _, part = plan[half, label]
             ring(half, label, src, part, label in (0, 1, 4, 5)).wait_send()
-    for save, (share, theirs) in zip(saved, shared):
-        save.wait()
+    for share, theirs in shared:
         share.wait_send()
         theirs.wait_recv()
 
 
-def attend_kernel(q, kv, cot, col_block, col_count, out, dqt, own, sib, total):
+def attend_kernel(q, kv, cot, col_block, col_count, out, dqt, total):
     clus, fsdp, core = here()
     total[...] = jnp.zeros_like(total)
 
-    def step(i, carry):
+    def stage_one(i):
         block = 2 * NZ * i + 2 * fsdp + core
-        cols = [col_block[block, k] for k in range(NCOL)]
+        cols = [col_block[k, block] for k in range(NCOL)]
         cols = [(c // (2 * NZ)) * 2 + c % 2 for c in cols]
-        count = col_count[block]
+        live = col_count[block] == NCOL
         query, grad = q[i], cot[i]
-        keys = jnp.concatenate([kv[c, 0] for c in cols], axis=0)
+        pair = jnp.concatenate([query, grad], axis=0)
+        both = [
+            lax.dot_general(kv[c, 0], pair, NT, preferred_element_type=F32) for c in cols
+        ]
+        return cols, live, query, grad, both
+
+    def stage_two(cols, live, query, grad, both):
+        scores = [x[:, :BLK] for x in both]
+        scores[-1] = jnp.where(live, scores[-1], -1e30)
+        top = functools.reduce(jnp.maximum, scores)
+        top = jnp.max(top, axis=0, keepdims=True)
+        expos = [jnp.exp2((x - top) * LOG2) for x in scores]
+        norm = jnp.sum(functools.reduce(jnp.add, expos), axis=0, keepdims=True)
+        inv = 1.0 / norm
+        probs = [x * inv for x in expos]
+        delta = functools.reduce(jnp.add, [p * x[:, BLK:] for p, x in zip(probs, both)])
+        delta = jnp.sum(delta, axis=0, keepdims=True)
+        ds = [(p * SCALE * (x[:, BLK:] - delta)).astype(BF) for p, x in zip(probs, both)]
+        return ds, [p.astype(BF) for p in probs]
+
+    def stage_three(i, cols, query, grad, ds, pb):
         keys_t = jnp.concatenate([kv[c, 1] for c in cols], axis=1)
-        both = lax.dot_general(
-            keys, jnp.concatenate([query, grad], axis=0), NT, preferred_element_type=F32
-        )
-        score = both[:, :BLK] * SCALE
-        dprob = both[:, BLK:]
-        place = lax.broadcasted_iota(jnp.int32, score.shape, 0) // BLK
-        score = jnp.where(place < count, score, -1e30)
-        top = jnp.max(score, axis=0, keepdims=True)
-        expo = jnp.exp(score - top)
-        prob = expo * (1.0 / jnp.sum(expo, axis=0, keepdims=True))
-        delta = jnp.sum(prob * dprob, axis=0, keepdims=True)
-        dscore = (prob * (dprob - delta)).astype(BF)
-        prob_b = prob.astype(BF)
-        both_t = lax.dot_general(
-            keys_t,
-            jnp.concatenate([dscore, prob_b], axis=1),
-            NN,
-            preferred_element_type=F32,
-        )
-        dqt[:, pl.ds(pl.multiple_of(i * BLK, BLK), BLK)] = (both_t[:, :BLK] * SCALE).astype(BF)
+        right = jnp.concatenate(
+            [jnp.concatenate(ds, axis=0), jnp.concatenate(pb, axis=0)], axis=1
+        )
+        both_t = lax.dot_general(keys_t, right, NN, preferred_element_type=F32)
+        dqt[:, pl.ds(pl.multiple_of(i * BLK, BLK), BLK)] = both_t[:, :BLK].astype(BF)
         out[i] = both_t[:, BLK:].T.astype(BF)
-        dkeys = (
-            lax.dot_general(dscore, query, NN, preferred_element_type=F32) * SCALE
-            + lax.dot_general(prob_b, grad, NN, preferred_element_type=F32)
-        )
+        pair = jnp.concatenate([query, grad], axis=0)
         for k, c in enumerate(cols):
-            total[c // 2, c % 2] += dkeys[k * BLK : (k + 1) * BLK]
+            total[c // 2, c % 2] += lax.dot_general(
+                jnp.concatenate([ds[k], pb[k]], axis=1), pair, NN, preferred_element_type=F32
+            )
+
+    GROUP = 4
+
+    def step(n, carry):
+        items = [n * GROUP + g for g in range(GROUP)]
+        ones = [stage_one(i) for i in items]
+        twos = [stage_two(*o) for o in ones]
+        for i, o, t in zip(items, ones, twos):
+            stage_three(i, o[0], o[2], o[3], *t)
         return carry
 
-    lax.fori_loop(0, NC, step, 0, unroll=2)
-    own[...] = total[:, core]
-    sib[...] = total[:, 1 - core].astype(BF)
+    lax.fori_loop(0, NC // GROUP, step, 0)
 
 
 def scatter_kernel(
     feats,
     out_blocks,
     dqt,
-    own,
-    sib,
+    dkv,
     out,
     grad_q,
     grad_k,
-    rows,
     other,
     dkt,
     part_send,
@@ -426,7 +432,6 @@
     z_out,
     z_in,
     fin,
-    load_sem,
     dk_sem,
     out_send,
     out_recv,
@@ -438,31 +443,20 @@
     fin_recv,
 ):
     clus, fsdp, core = here()
-    CH = 256
-    NCH = D // CH
-    greet_all(clus, fsdp, core)
-    give = remote(sib, other, dk_sem.at[0], dk_sem.at[1], (clus, fsdp, 1 - core))
-    give.start()
-
-    def chunk(n):
-        return (n + (1 - core) * (NCH // 2)) % NCH
-
-    def load(n):
-        cols = pl.ds(pl.multiple_of(chunk(n) * CH, CH), CH)
-        return pltpu.make_async_copy(
-            feats.at[:, :, cols], rows.at[:, :, cols], load_sem.at[n]
-        )
-
-    for n in range(NCH):
-        load(n).start()
+    greet(clus, fsdp, core)
+    sibling = (clus, fsdp, 1 - core)
+    give = remote(dkv.at[:, 1 - core], other, dk_sem.at[0], dk_sem.at[1], sibling)
+
+    def out_spot():
+        return out.at[
+            pl.ds(pl.multiple_of(core * BLK, BLK), BLK),
+            pl.ds(pl.multiple_of((clus % PER) * HD, HD), HD),
+        ]
 
     def out_copy(s):
         return remote(
             out_blocks.at[s],
-            out.at[
-                pl.ds(pl.multiple_of(core * BLK, BLK), BLK),
-                pl.ds(pl.multiple_of((clus % PER) * HD, HD), HD),
-            ],
+            out_spot(),
             out_send.at[s],
             out_recv.at[2 * (clus % PER) + core],
             (s, fsdp, clus // PER),
@@ -470,81 +464,85 @@
 
     own_out = core == clus // PER
 
-    @pl.loop(0, NC)
-    def _(i):
-        s = (i + clus) % NC
-        mine = jnp.logical_and(s == clus, own_out)
-
-        @pl.when(mine)
-        def _():
-            pltpu.make_async_copy(
-                out_blocks.at[s],
-                out.at[
-                    pl.ds(pl.multiple_of(core * BLK, BLK), BLK),
-                    pl.ds(pl.multiple_of((clus % PER) * HD, HD), HD),
-                ],
-                out_recv.at[2 * (clus % PER) + core],
-            ).start()
-
-        @pl.when(jnp.logical_not(mine))
-        def _():
-            out_copy(s).start()
+    def send_out():
+        @pl.loop(0, NC)
+        def _(i):
+            s = (i + clus) % NC
+            mine = jnp.logical_and(s == clus, own_out)
+
+            @pl.when(mine)
+            def _():
+                pltpu.make_async_copy(
+                    out_blocks.at[s], out_spot(), out_recv.at[2 * (clus % PER) + core]
+                ).start()
+
+            @pl.when(jnp.logical_not(mine))
+            def _():
+                out_copy(s).start()
 
     def half_copy(t):
         return remote(
-            part_send.at[t],
-            part_recv.at[t],
-            half_send.at[t],
-            half_recv.at[t],
-            (clus, fsdp, 1 - core),
-        )
-
-    def z_copy(t, i):
+            part_send.at[t], part_recv.at[t], half_send.at[t], half_recv.at[t], sibling
+        )
+
+    def z_copy(t, g, i):
         to = (fsdp + i) % NZ
         return remote(
-            z_out.at[t, to],
-            z_in.at[t, fsdp],
-            z_send.at[t, i],
-            z_recv.at[t, i],
+            z_out.at[t, g, to],
+            z_in.at[t, g, fsdp],
+            z_send.at[2 * t + g, i],
+            z_recv.at[2 * t + g, i],
             (clus, to, core),
         )
 
-    def gradient(t, lhs):
-        for n in range(NCH):
-            if t == 0:
-                load(n).wait()
-            cols = pl.ds(pl.multiple_of(chunk(n) * CH, CH), CH)
-            part = lax.dot_general(
-                lhs[...],
-                rows[:, :, cols].reshape(NC * BLK, CH),
-                NN,
-                preferred_element_type=F32,
-            )
-            for k in range(CH // BLK):
-                piece = part[:, k * BLK : (k + 1) * BLK].T.reshape(NZ, WROWS, HD)
-                index = (n * CH) // BLK + k
-                if index < PER:
-                    part_send[t, index] = piece.astype(BF)
-                else:
-                    part_own[t, index - PER] = piece
-            if n == NCH // 2 - 1:
-                half_copy(t).start()
-        half_copy(t).wait_recv()
-        for k in range(PER):
-            total = part_own[t, k] + part_recv[t, k].astype(F32)
-            part_own[t, k] = total
-            z_out[t, :, k] = total.astype(BF)
-
-        @pl.loop(1, NZ)
-        def _(i):
-            z_copy(t, i).start()
-
-    gradient(0, dqt)
+    CH = 2 * BLK
+
+    def chunk(lhs, n, side):
+        cols = pl.ds(pl.multiple_of(side * HALF + n * CH, CH), CH)
+        part = lax.dot_general(
+            lhs[...],
+            feats[:, :, cols].reshape(NC * BLK, CH),
+            NN,
+            preferred_element_type=F32,
+        )
+        return [part[:, k * BLK : (k + 1) * BLK].T.reshape(NZ, WROWS, HD) for k in (0, 1)]
+
+    def for_sibling(t, lhs):
+        for n in range(PER // 2):
+            for k, piece in enumerate(chunk(lhs, n, 1 - core)):
+                part_send[t, 2 * n + k] = piece.astype(BF)
+
+    def for_self(t, lhs):
+        for n in range(PER // 2):
+            for k, piece in enumerate(chunk(lhs, n, core)):
+                part_own[t, 2 * n + k] = piece
+            if n == 1:
+                half_copy(t).wait_recv()
+            if n % 2 == 1:
+                g = n // 2
+                for k in range(PER // 2):
+                    at = g * (PER // 2) + k
+                    total = part_own[t, at] + part_recv[t, at].astype(F32)
+                    part_own[t, at] = total
+                    z_out[t, g, :, k] = total.astype(BF)
+
+                @pl.loop(1, NZ)
+                def _(i):
+                    z_copy(t, g, i).start()
+
+    for_sibling(0, dqt)
+    greeted()
+    give.start()
+    half_copy(0).start()
+    for_self(0, dqt)
     give.wait_recv()
     for s in range(NC):
-        total = own[s] + other[s].astype(F32)
-        dkt[:, s * BLK : (s + 1) * BLK] = total.astype(BF).astype(F32).T.astype(BF)
-    gradient(1, dkt)
+        total = (dkv[s, core] + other[s]).astype(BF).astype(F32)
+        dkt[:, s * BLK : (s + 1) * BLK] = total.T.astype(BF)
+    for_sibling(1, dkt)
+    half_copy(1).start()
+    for_self(1, dkt)
+    send_out()
 
     def fin_copy(t, k):
         dest = (grad_q, grad_k)[t]
@@ -557,38 +555,40 @@
         )
 
     for t in (0, 1):
-        for i in range(1, NZ):
-            frm = (fsdp + NZ - i) % NZ
-            remote(
-                z_out.at[t, 0],
-                z_in.at[t, frm],
-                z_send.at[t, i],
-                z_recv.at[t, i],
-                (clus, frm, core),
-            ).wait_recv()
-        for k in range(PER):
-            total = part_own[t, k, fsdp]
+        for g in (0, 1):
             for i in range(1, NZ):
-                total += z_in[t, (fsdp + NZ - i) % NZ, k].astype(F32)
-            fin[t, k] = total
-        for k in range(PER):
-            to, src, dst, recv = fin_copy(t, k)
-
-            @pl.when(to == clus)
-            def _():
-                pltpu.make_async_copy(src, dst, recv).start()
-
-            @pl.when(to != clus)
-            def _():
-                remote(src, dst, fin_send.at[t, k], recv, (to, fsdp, clus // PER)).start()
+                frm = (fsdp + NZ - i) % NZ
+                remote(
+                    z_out.at[t, g, 0],
+                    z_in.at[t, g, frm],
+                    z_send.at[2 * t + g, i],
+                    z_recv.at[2 * t + g, i],
+                    (clus, frm, core),
+                ).wait_recv()
+            for k in range(PER // 2):
+                at = g * (PER // 2) + k
+                total = part_own[t, at, fsdp]
+                for i in range(1, NZ):
+                    total += z_in[t, g, (fsdp + NZ - i) % NZ, k].astype(F32)
+                fin[t, at] = total
+                to, src, dst, recv = fin_copy(t, at)
+
+                @pl.when(to == clus)
+                def _():
+                    pltpu.make_async_copy(src, dst, recv).start()
+
+                @pl.when(to != clus)
+                def _():
+                    remote(src, dst, fin_send.at[t, at], recv, (to, fsdp, clus // PER)).start()
 
     give.wait_send()
     for t in (0, 1):
         half_copy(t).wait_send()
-
-        @pl.loop(1, NZ)
-        def _(i):
-            z_copy(t, i).wait_send()
+        for g in (0, 1):
+
+            @pl.loop(1, NZ)
+            def _(i):
+                z_copy(t, g, i).wait_send()
 
         for k in range(PER):
             to, src, dst, recv = fin_copy(t, k)
@@ -610,7 +610,7 @@
                 out.at[pl.ds(block * BLK, BLK), pl.ds(m * HD, HD)],
                 out_send.at[0],
                 out_recv.at[2 * m + block],
-                (clus, fsdp, 1 - core),
+                sibling,
             ).wait_recv()
         for t in (0, 1):
             remote(
@@ -618,15 +618,15 @@
                 (grad_q, grad_k)[t].at[:, pl.ds(m * HD, HD)],
                 fin_send.at[t, 0],
                 fin_recv.at[t, m],
-                (clus, fsdp, 1 - core),
+                sibling,
             ).wait_recv()
 
 
-ANY = pl.BlockSpec(memory_space=pl.ANY)
+HB = pl.BlockSpec(memory_space=pltpu.HBM)
 VM = pl.BlockSpec(memory_space=pltpu.VMEM)
 SM = pl.BlockSpec(memory_space=pltpu.SMEM)
 DMA = pltpu.SemaphoreType.DMA
-LIMIT = 56 * 1024 * 1024
+MIB = 1 << 20
 
 
 def shape(dims, kind):
@@ -643,16 +643,14 @@
             shape((2 * NC, 2, BLK, HD), BF),
             shape((NC, BLK, HD), BF),
         ),
-        in_specs=[ANY, VM, VM, ANY],
-        out_specs=(ANY, VM, VM, VM),
+        in_specs=[HB, VM, VM, HB],
+        out_specs=(VM, VM, VM, VM),
         scratch_shapes=[
-            pltpu.VMEM((NC, BLK, D), BF),
             pltpu.VMEM((2, WROWS, HALF), BF),
             pltpu.VMEM((2, NC, NZ, WROWS, HD), BF),
             DMA((40,)),
             DMA((40,)),
             DMA,
-            DMA((NC,)),
             DMA((16,)),
             DMA((NC,)),
             DMA((NZ,)),
@@ -665,29 +663,27 @@
             DMA((NC,)),
         ],
         compiler_params=pltpu.CompilerParams(
-            collective_id=1, has_side_effects=True, vmem_limit_bytes=LIMIT
+            collective_id=1, has_side_effects=True, vmem_limit_bytes=24 * MIB
         ),
         cost_estimate=pl.CostEstimate(
             flops=2 * D * D * 256, bytes_accessed=18 << 20, transcendentals=0
         ),
     )(feats, w_query, w_keyval, grad_out)
-    out_blocks, dqt, own, sib = pl.pallas_call(
+    out_blocks, dqt, dkv = pl.pallas_call(
         attend_kernel,
         name="attend",
         out_shape=(
             shape((NC, BLK, HD), BF),
             shape((HD, NC * BLK), BF),
-            shape((NC, BLK, HD), F32),
-            shape((NC, BLK, HD), BF),
+            shape((NC, 2, BLK, HD), F32),
         ),
         in_specs=[VM, VM, VM, SM, SM],
-        out_specs=(VM, VM, VM, VM),
-        scratch_shapes=[pltpu.VMEM((NC, 2, BLK, HD), F32)],
-        compiler_params=pltpu.CompilerParams(vmem_limit_bytes=LIMIT),
+        out_specs=(VM, VM, VM),
+        compiler_params=pltpu.CompilerParams(vmem_limit_bytes=16 * MIB),
         cost_estimate=pl.CostEstimate(
-            flops=12 * NC * BLK * 640 * HD, bytes_accessed=6 << 20, transcendentals=NC * BLK * 640
-        ),
-    )(query, keyval, cots, col_block, col_count)
+            flops=12 * NC * BLK * 640 * HD, bytes_accessed=6 * MIB, transcendentals=NC * BLK * 640
+        ),
+    )(query, keyval, cots, col_block.T, col_count)
     return pl.pallas_call(
         scatter_kernel,
         name="scatter_grads",
@@ -696,36 +692,34 @@
             shape((WROWS, HALF), F32),
             shape((WROWS, HALF), F32),
         ),
-        in_specs=[ANY, VM, VM, VM, VM],
+        in_specs=[VM, VM, VM, VM],
         out_specs=(VM, VM, VM),
         scratch_shapes=[
-            pltpu.VMEM((NC, BLK, D), BF),
-            pltpu.VMEM((NC, BLK, HD), BF),
+            pltpu.VMEM((NC, BLK, HD), F32),
             pltpu.VMEM((HD, NC * BLK), BF),
             pltpu.VMEM((2, PER, NZ, WROWS, HD), BF),
             pltpu.VMEM((2, PER, NZ, WROWS, HD), BF),
             pltpu.VMEM((2, PER, NZ, WROWS, HD), F32),
-            pltpu.VMEM((2, NZ, PER, WROWS, HD), BF),
-            pltpu.VMEM((2, NZ, PER, WROWS, HD), BF),
+            pltpu.VMEM((2, 2, NZ, PER // 2, WROWS, HD), BF),
+            pltpu.VMEM((2, 2, NZ, PER // 2, WROWS, HD), BF),
             pltpu.VMEM((2, PER, WROWS, HD), F32),
-            DMA((8,)),
             DMA((2,)),
             DMA((NC,)),
             DMA((NC,)),
             DMA((2,)),
             DMA((2,)),
-            DMA((2, NZ)),
-            DMA((2, NZ)),
+            DMA((4, NZ)),
+            DMA((4, NZ)),
             DMA((2, PER)),
             DMA((2, PER)),
         ],
         compiler_params=pltpu.CompilerParams(
-            collective_id=2, has_side_effects=True, vmem_limit_bytes=LIMIT
+            collective_id=2, has_side_effects=True, vmem_limit_bytes=24 * MIB
         ),
         cost_estimate=pl.CostEstimate(
-            flops=2 * D * D * 256, bytes_accessed=12 << 20, transcendentals=0
-        ),
-    )(feats_all, out_blocks, dqt, own, sib)
+            flops=2 * D * D * 256, bytes_accessed=12 * MIB, transcendentals=0
+        ),
+    )(feats_all, out_blocks, dqt, dkv)
 
 
 def solution(mesh):

time: 124 us -> 105 us (0.85)
  Pallas kernels: 117 us -> 96.9 us
    pallas_call x1, Pallas kernels: 17.7 us -> 7.66 us  [on_device(): pl.pallas_call(attend_kernel, name='attend', out_shape=(shape((NC, BLK, H...]
    pallas_call x1, Pallas kernels: 31.3 us -> 24.8 us  [on_device(): pl.pallas_call(scatter_kernel, name='scatter_grads', out_shape=(shape((2...]
    pallas_call x1, Pallas kernels: 67.6 us -> 64.5 us  [on_device(): pl.pallas_call(gather_kernel, name='gather_project', out_shape=(shape((NC...]
    unnamed x4 -> x15, local copies, waits for them, and re-layouts: 6.3 us -> 6 us
where the time goes in v2:
time: 105 us; the launch traced here: 104 us
  Pallas kernels  96.9 us (92%)
  local copies, waits for them, and re-layouts  6 us (6%)
    pallas_call x1, Pallas kernels, on_device(): pl.pallas_call(gather_kernel, name='gather_project', out_shape=(shape((NC...  64.5 us
    pallas_call x1, Pallas kernels, on_device(): pl.pallas_call(scatter_kernel, name='scatter_grads', out_shape=(shape((2...  24.8 us
    pallas_call x1, Pallas kernels, on_device(): pl.pallas_call(attend_kernel, name='attend', out_shape=(shape((NC, BLK, H...  7.66 us
    unnamed x15, local copies, waits for them, and re-layouts  6 us

profile of v2, /device:TPU:1, one launch (start us, length us, event | category | flops | bytes accessed | tf_op | source)
XLA Modules:
  0.0 103.6 jit_solution(18128396568655536388)
XLA Ops:
  0.6 0.0 copy-start
  0.6 1.2 %copy-done = bf16[256,2048]{1,0:T(8,128)(2,1)S(1)} copy-done((bf16[256,2048]{1,0:T(8,128)(2,1)S(1)}, bf16[256,2048]{1,0:T(8,128)(2,1)}, u32[]{:S(2)}) %copy-start) | copy-done | bytes 1048600
  1.9 0.0 copy-start.1
  1.9 1.0 %copy-done.1 = bf16[256,1024]{1,0:T(8,128)(2,1)S(1)} copy-done((bf16[256,1024]{1,0:T(8,128)(2,1)S(1)}, bf16[256,1024]{1,0:T(8,128)(2,1)}, u32[]{:S(2)}) %copy-start.1) | copy-done | bytes 524312
  2.9 0.0 copy-start.2
  2.9 0.8 copy-done.2
  3.7 0.0 copy-start.3
  3.7 0.8 copy-done.3
  4.6 0.0 copy-start.4
  4.6 0.0 copy-start.5
  4.6 64.5 %gather_project.1 = (bf16[16,128,2048]{2,1,0:T(8,128)(2,1)S(1)}, bf16[16,128,128]{2,1,0:T(8,128)(2,1)S(1)}, bf16[32,2,128,128]{3,2,1,0:T(8,128)(2,1)S(1)}, bf16[16,128,128]{2,1,0:T(8,128)(2,1)S(1)}) custom-call(bf16[256,2048]{1,0:T(8,128)(2,1)S(1)} %copy-done, f32[16,1024]{1,0:T(8,128)S(1)} %copy-done.2, f32[16,1024]{1,0:T(8,128)S(1)} %copy-done.3, ...), custom_call_target="tpu_custom_call" | custom-call | flops 2147483648 | bytes 18874368 | tf_op jit(solution)/shard_map/gather_project/pallas_call | solution.py:637
  69.1 0.0 copy-done.4
  69.1 0.0 copy-done.5
  69.1 7.7 %attend.1 = (bf16[16,128,128]{2,1,0:T(8,128)(2,1)S(1)}, bf16[128,2048]{1,0:T(8,128)(2,1)S(1)}, f32[16,2,128,128]{3,2,1,0:T(8,128)S(1)}) custom-call(bf16[16,128,128]{2,1,0:T(8,128)(2,1)S(1)} %get-tuple-element.11.q, bf16[32,2,128,128]{3,2,1,0:T(8,128)(2,1)S(1)} %get-tuple-element.12.kv, bf16[16,128,128]{2,1,0:T(8,128)(2,1)S(1)} %get-tuple-element.13.cot, ...), custom_call_target="tpu_custom_call" | custom-call | flops 2013265920 | bytes 6291456 | tf_op jit(solution)/shard_map/attend/pallas_call | solution.py:672
  76.7 24.8 %scatter_grads.1 = (bf16[256,1024]{1,0:T(8,128)(2,1)S(1)}, f32[16,1024]{1,0:T(8,128)S(1)}, f32[16,1024]{1,0:T(8,128)S(1)}) custom-call(bf16[16,128,2048]{2,1,0:T(8,128)(2,1)S(1)} %get-tuple-element.10.feats, bf16[16,128,128]{2,1,0:T(8,128)(2,1)S(1)} %get-tuple-element.14.out_blocks, bf16[128,2048]{1,0:T(8,128)(2,1)S(1)} %get-tuple-element.15.dqt, ...), custom_call_target="tpu_custom_call" | custom-call | flops 2147483648 | bytes 12582912 | tf_op jit(solution)/shard_map/scatter_grads/pallas_call | solution.py:687
  101.5 0.8 copy.12
  102.3 0.6 copy.13
  102.9 0.6 copy.14
Async XLA Ops:
  0.6 1.2 %copy-start = (bf16[256,2048]{1,0:T(8,128)(2,1)S(1)}, bf16[256,2048]{1,0:T(8,128)(2,1)}, u32[]{:S(2)}) copy-start(bf16[256,2048]{1,0:T(8,128)(2,1)} %feats.1) | copy-start | bytes 3145732
  1.9 1.0 %copy-start.1 = (bf16[256,1024]{1,0:T(8,128)(2,1)S(1)}, bf16[256,1024]{1,0:T(8,128)(2,1)}, u32[]{:S(2)}) copy-start(bf16[256,1024]{1,0:T(8,128)(2,1)} %grad_out.1) | copy-start | bytes 1572868
  2.9 0.8 copy-start.2
  3.7 0.8 copy-start.3
  4.6 64.5 %copy-start.4 = (s32[256,5]{0,1:T(8,128)S(1)}, s32[256,5]{0,1:T(8,128)}, u32[]{:S(2)}) copy-start(s32[256,5]{0,1:T(8,128)} %param.10) | copy-start | bytes 15364
  4.6 64.5 %copy-start.5 = (s32[256]{0:T(256)S(1)}, s32[256]{0:T(256)}, u32[]{:S(2)}) copy-start(s32[256]{0:T(256)} %col_count.1) | copy-start | bytes 3076

commit v3 on v2

--- a/solution.py
+++ b/solution.py
@@ -77,8 +77,10 @@
     q_out,
     kv_out,
     cot_out,
+    wf,
     wb,
     wall,
+    wf_sem,
     ring_send,
     ring_recv,
     local_sem,
@@ -99,9 +101,16 @@
     def at(dx, dy):
         return ((yp + dy) % SIDE) * SIDE + (xp + dx) % SIDE
 
+    loads = [
+        pltpu.make_async_copy(w, wf.at[part], wf_sem.at[part])
+        for part, w in enumerate((w_query, w_keyval))
+    ]
+    for load in loads:
+        load.start()
     greet(clus, fsdp, core)
-    wb[0] = w_query[...].astype(BF)
-    wb[1] = w_keyval[...].astype(BF)
+    for part, load in enumerate(loads):
+        load.wait()
+        wb[part] = wf[part].astype(BF)
     greeted()
 
     def slot(half, first, second):
@@ -216,6 +225,9 @@
         ]
         return head, src, cot_out.at[clus]
 
+    arrived(0, 1)
+    send(2, 3, 8, 9, 12, 13)
+
     @pl.loop(0, PER)
     def _(i):
         j = (i + clus) % PER
@@ -233,8 +245,6 @@
                     src, dst, cot_send.at[2 * j + block], cot_recv.at[clus], (head, fsdp, block)
                 ).start()
 
-    arrived(0, 1)
-    send(2, 3, 8, 9, 12, 13)
 
     @pl.loop(1, NZ)
     def _(i):
@@ -485,15 +495,36 @@
             part_send.at[t], part_recv.at[t], half_send.at[t], half_recv.at[t], sibling
         )
 
-    def z_copy(t, g, i):
-        to = (fsdp + i) % NZ
+    HOPS = ((-2, -4), (-1, -3), (1, 3), (-1, -1), (1, 1), (-2, -2), (2, 2))
+
+    def turn(t, steps):
+        return (fsdp + NZ + (steps if t == 0 else -steps)) % NZ
+
+    def z_copy(t, i):
+        hops, owner = HOPS[i]
         return remote(
-            z_out.at[t, g, to],
-            z_in.at[t, g, fsdp],
-            z_send.at[2 * t + g, i],
-            z_recv.at[2 * t + g, i],
-            (clus, to, core),
-        )
+            z_out.at[t, turn(t, owner)],
+            z_in.at[t, i],
+            z_send.at[t, i],
+            z_recv.at[t, i],
+            (clus, turn(t, hops), core),
+        )
+
+    def stage_one(t):
+        for i in range(5):
+            z_copy(t, i).start()
+
+    def stage_two(t):
+        for i in range(3):
+            z_copy(t, i).wait_recv()
+        down, up = turn(t, -2), turn(t, 2)
+        for k in range(PER):
+            total = part_own[t, k, down] + z_in[t, 0, k].astype(F32) + z_in[t, 1, k].astype(F32)
+            z_out[t, down, k] = total.astype(BF)
+        z_copy(t, 5).start()
+        for k in range(PER):
+            z_out[t, up, k] = (part_own[t, k, up] + z_in[t, 2, k].astype(F32)).astype(BF)
+        z_copy(t, 6).start()
 
     CH = 2 * BLK
 
@@ -516,25 +547,22 @@
         for n in range(PER // 2):
             for k, piece in enumerate(chunk(lhs, n, core)):
                 part_own[t, 2 * n + k] = piece
-            if n == 1:
-                half_copy(t).wait_recv()
-            if n % 2 == 1:
-                g = n // 2
-                for k in range(PER // 2):
-                    at = g * (PER // 2) + k
-                    total = part_own[t, at] + part_recv[t, at].astype(F32)
-                    part_own[t, at] = total
-                    z_out[t, g, :, k] = total.astype(BF)
-
-                @pl.loop(1, NZ)
-                def _(i):
-                    z_copy(t, g, i).start()
+
+    def add_sibling(t):
+        half_copy(t).wait_recv()
+        for k in range(PER):
+            total = part_own[t, k] + part_recv[t, k].astype(F32)
+            part_own[t, k] = total
+            z_out[t, :, k] = total.astype(BF)
+        stage_one(t)
 
     for_sibling(0, dqt)
+    for_self(0, dqt)
     greeted()
+    half_copy(0).start()
     give.start()
-    half_copy(0).start()
-    for_self(0, dqt)
+    send_out()
+    add_sibling(0)
     give.wait_recv()
     for s in range(NC):
         total = (dkv[s, core] + other[s]).astype(BF).astype(F32)
@@ -542,7 +570,9 @@
     for_sibling(1, dkt)
     half_copy(1).start()
     for_self(1, dkt)
-    send_out()
+    add_sibling(1)
+    stage_two(0)
+    stage_two(1)
 
     def fin_copy(t, k):
         dest = (grad_q, grad_k)[t]
@@ -555,42 +585,36 @@
         )
 
     for t in (0, 1):
-        for g in (0, 1):
-            for i in range(1, NZ):
-                frm = (fsdp + NZ - i) % NZ
-                remote(
-                    z_out.at[t, g, 0],
-                    z_in.at[t, g, frm],
-                    z_send.at[2 * t + g, i],
-                    z_recv.at[2 * t + g, i],
-                    (clus, frm, core),
-                ).wait_recv()
-            for k in range(PER // 2):
-                at = g * (PER // 2) + k
-                total = part_own[t, at, fsdp]
-                for i in range(1, NZ):
-                    total += z_in[t, g, (fsdp + NZ - i) % NZ, k].astype(F32)
-                fin[t, at] = total
-                to, src, dst, recv = fin_copy(t, at)
-
-                @pl.when(to == clus)
-                def _():
-                    pltpu.make_async_copy(src, dst, recv).start()
-
-                @pl.when(to != clus)
-                def _():
-                    remote(src, dst, fin_send.at[t, at], recv, (to, fsdp, clus // PER)).start()
+        for i in range(3, 7):
+            z_copy(t, i).wait_recv()
+        for k in range(PER):
+            total = part_own[t, k, fsdp]
+            for i in range(3, 7):
+                total += z_in[t, i, k].astype(F32)
+            fin[t, k] = total
+
+        @pl.loop(0, PER)
+        def _(i):
+            k = (i + clus) % PER
+            to, src, dst, recv = fin_copy(t, k)
+
+            @pl.when(to == clus)
+            def _():
+                pltpu.make_async_copy(src, dst, recv).start()
+
+            @pl.when(to != clus)
+            def _():
+                remote(src, dst, fin_send.at[t, k], recv, (to, fsdp, clus // PER)).start()
 
     give.wait_send()
     for t in (0, 1):
         half_copy(t).wait_send()
-        for g in (0, 1):
-
-            @pl.loop(1, NZ)
-            def _(i):
-                z_copy(t, g, i).wait_send()
-
-        for k in range(PER):
+        for i in range(7):
+            z_copy(t, i).wait_send()
+
+
+        @pl.loop(0, PER)
+        def _(k):
             to, src, dst, recv = fin_copy(t, k)
 
             @pl.when(to != clus)
@@ -622,6 +646,16 @@
             ).wait_recv()
 
 
+def place_kernel(*refs):
+    copies = [
+        pltpu.make_async_copy(refs[i], refs[3 + i], refs[6].at[i]) for i in range(3)
+    ]
+    for copy in copies:
+        copy.start()
+    for copy in copies:
+        copy.wait()
+
+
 HB = pl.BlockSpec(memory_space=pltpu.HBM)
 VM = pl.BlockSpec(memory_space=pltpu.VMEM)
 SM = pl.BlockSpec(memory_space=pltpu.SMEM)
@@ -643,11 +677,13 @@
             shape((2 * NC, 2, BLK, HD), BF),
             shape((NC, BLK, HD), BF),
         ),
-        in_specs=[HB, VM, VM, HB],
+        in_specs=[HB, HB, HB, HB],
         out_specs=(VM, VM, VM, VM),
         scratch_shapes=[
+            pltpu.VMEM((2, WROWS, HALF), F32),
             pltpu.VMEM((2, WROWS, HALF), BF),
             pltpu.VMEM((2, NC, NZ, WROWS, HD), BF),
+            DMA((2,)),
             DMA((40,)),
             DMA((40,)),
             DMA,
@@ -668,7 +704,7 @@
         cost_estimate=pl.CostEstimate(
             flops=2 * D * D * 256, bytes_accessed=18 << 20, transcendentals=0
         ),
-    )(feats, w_query, w_keyval, grad_out)
+    )(*(pltpu.with_memory_space_constraint(x, pltpu.HBM) for x in (feats, w_query, w_keyval, grad_out)))
     out_blocks, dqt, dkv = pl.pallas_call(
         attend_kernel,
         name="attend",
@@ -684,7 +720,7 @@
             flops=12 * NC * BLK * 640 * HD, bytes_accessed=6 * MIB, transcendentals=NC * BLK * 640
         ),
     )(query, keyval, cots, col_block.T, col_count)
-    return pl.pallas_call(
+    results = pl.pallas_call(
         scatter_kernel,
         name="scatter_grads",
         out_shape=(
@@ -700,16 +736,16 @@
             pltpu.VMEM((2, PER, NZ, WROWS, HD), BF),
             pltpu.VMEM((2, PER, NZ, WROWS, HD), BF),
             pltpu.VMEM((2, PER, NZ, WROWS, HD), F32),
-            pltpu.VMEM((2, 2, NZ, PER // 2, WROWS, HD), BF),
-            pltpu.VMEM((2, 2, NZ, PER // 2, WROWS, HD), BF),
+            pltpu.VMEM((2, NZ, PER, WROWS, HD), BF),
+            pltpu.VMEM((2, 7, PER, WROWS, HD), BF),
             pltpu.VMEM((2, PER, WROWS, HD), F32),
             DMA((2,)),
             DMA((NC,)),
             DMA((NC,)),
             DMA((2,)),
             DMA((2,)),
-            DMA((4, NZ)),
-            DMA((4, NZ)),
+            DMA((2, 7)),
+            DMA((2, 7)),
             DMA((2, PER)),
             DMA((2, PER)),
         ],
@@ -720,6 +756,15 @@
             flops=2 * D * D * 256, bytes_accessed=12 * MIB, transcendentals=0
         ),
     )(feats_all, out_blocks, dqt, dkv)
+    return pl.pallas_call(
+        place_kernel,
+        name="place",
+        out_shape=tuple(pltpu.HBM(r.shape, r.dtype) for r in results),
+        in_specs=[VM] * 3,
+        out_specs=(HB,) * 3,
+        scratch_shapes=[DMA((3,))],
+        compiler_params=pltpu.CompilerParams(vmem_limit_bytes=16 * MIB),
+    )(*results)
 
 
 def solution(mesh):

time: 105 us -> 98.2 us (0.935); the launches traced: 104 us -> 98.1 us
  local copies, waits for them, and re-layouts: 6 us -> 0.01 us
    unnamed x15 -> x4, local copies, waits for them, and re-layouts: 6 us -> 0.01 us
where the time goes in v3:
time: 98.2 us; the launch traced here: 98.1 us
  Pallas kernels  97.4 us (99%)
    pallas_call x1, Pallas kernels, on_device(): pl.pallas_call(gather_kernel, name='gather_project', out_shape=(shape((NC...  64.9 us
    pallas_call x1, Pallas kernels, on_device(): pl.pallas_call(scatter_kernel, name='scatter_grads', out_shape=(shape((2...  23.9 us
    pallas_call x1, Pallas kernels, on_device(): pl.pallas_call(attend_kernel, name='attend', out_shape=(shape((NC, BLK, H...  7.68 us

profile of v3, /device:TPU:1, one launch (start us, length us, event | category | flops | bytes accessed | tf_op | source)
XLA Modules:
  0.0 98.1 jit_solution(14476730720808308196)
XLA Ops:
  0.6 0.0 copy-start
  0.6 0.0 copy-start.1
  0.7 64.9 %gather_project.1 = (bf16[16,128,2048]{2,1,0:T(8,128)(2,1)S(1)}, bf16[16,128,128]{2,1,0:T(8,128)(2,1)S(1)}, bf16[32,2,128,128]{3,2,1,0:T(8,128)(2,1)S(1)}, bf16[16,128,128]{2,1,0:T(8,128)(2,1)S(1)}) custom-call(bf16[256,2048]{1,0:T(8,128)(2,1)} %feats.1, f32[16,1024]{1,0:T(8,128)} %w_query.1, f32[16,1024]{1,0:T(8,128)} %w_keyval.1, bf16[256,1024]{1,0:T(8,128)(2,1)} %grad_out.1), custom_call_target="tpu_custom_call" | custom-call | flops 2147483648 | bytes 18874368 | tf_op jit(solution)/shard_map/gather_project/pallas_call | solution.py:671
  65.6 0.0 copy-done
  65.6 0.0 copy-done.1
  65.6 7.7 %attend.1 = (bf16[16,128,128]{2,1,0:T(8,128)(2,1)S(1)}, bf16[128,2048]{1,0:T(8,128)(2,1)S(1)}, f32[16,2,128,128]{3,2,1,0:T(8,128)S(1)}) custom-call(bf16[16,128,128]{2,1,0:T(8,128)(2,1)S(1)} %get-tuple-element.14.q, bf16[32,2,128,128]{3,2,1,0:T(8,128)(2,1)S(1)} %get-tuple-element.15.kv, bf16[16,128,128]{2,1,0:T(8,128)(2,1)S(1)} %get-tuple-element.16.cot, ...), custom_call_target="tpu_custom_call" | custom-call | flops 2013265920 | bytes 6291456 | tf_op jit(solution)/shard_map/attend/pallas_call | solution.py:708
  73.3 23.9 %scatter_grads.1 = (bf16[256,1024]{1,0:T(8,128)(2,1)S(1)}, f32[16,1024]{1,0:T(8,128)S(1)}, f32[16,1024]{1,0:T(8,128)S(1)}) custom-call(bf16[16,128,2048]{2,1,0:T(8,128)(2,1)S(1)} %get-tuple-element.13.feats, bf16[16,128,128]{2,1,0:T(8,128)(2,1)S(1)} %get-tuple-element.17.out_blocks, bf16[128,2048]{1,0:T(8,128)(2,1)S(1)} %get-tuple-element.18.dqt, ...), custom_call_target="tpu_custom_call" | custom-call | flops 2147483648 | bytes 12582912 | tf_op jit(solution)/shard_map/scatter_grads/pallas_call | solution.py:723
  97.2 0.9 place.1
Async XLA Ops:
  0.6 65.0 %copy-start = (s32[256,5]{0,1:T(8,128)S(1)}, s32[256,5]{0,1:T(8,128)}, u32[]{:S(2)}) copy-start(s32[256,5]{0,1:T(8,128)} %param.10) | copy-start | bytes 15364
  0.6 65.0 %copy-start.1 = (s32[256]{0:T(256)S(1)}, s32[256]{0:T(256)}, u32[]{:S(2)}) copy-start(s32[256]{0:T(256)} %col_count.1) | copy-start | bytes 3076

commit v4 on v3

--- a/solution.py
+++ b/solution.py
@@ -413,7 +413,7 @@
                 jnp.concatenate([ds[k], pb[k]], axis=1), pair, NN, preferred_element_type=F32
             )
 
-    GROUP = 4
+    GROUP = 8
 
     def step(n, carry):
         items = [n * GROUP + g for g in range(GROUP)]

time: 98.2 us -> 97.9 us (level)
  no operation moved by 1% of the time
where the time goes in v4:
time: 97.9 us; the launch traced here: 97.8 us
  Pallas kernels  97.1 us (99%)
    pallas_call x1, Pallas kernels, on_device(): pl.pallas_call(gather_kernel, name='gather_project', out_shape=(shape((NC...  64.9 us
    pallas_call x1, Pallas kernels, on_device(): pl.pallas_call(scatter_kernel, name='scatter_grads', out_shape=(shape((2...  23.9 us
    pallas_call x1, Pallas kernels, on_device(): pl.pallas_call(attend_kernel, name='attend', out_shape=(shape((NC, BLK, H...  7.36 us

profile of v4, /device:TPU:1, one launch (start us, length us, event | category | flops | bytes accessed | tf_op | source)
XLA Modules:
  0.0 97.8 jit_solution(11256859002215775680)
XLA Ops:
  0.6 0.0 copy-start
  0.6 0.0 copy-start.1
  0.7 64.9 %gather_project.1 = (bf16[16,128,2048]{2,1,0:T(8,128)(2,1)S(1)}, bf16[16,128,128]{2,1,0:T(8,128)(2,1)S(1)}, bf16[32,2,128,128]{3,2,1,0:T(8,128)(2,1)S(1)}, bf16[16,128,128]{2,1,0:T(8,128)(2,1)S(1)}) custom-call(bf16[256,2048]{1,0:T(8,128)(2,1)} %feats.1, f32[16,1024]{1,0:T(8,128)} %w_query.1, f32[16,1024]{1,0:T(8,128)} %w_keyval.1, bf16[256,1024]{1,0:T(8,128)(2,1)} %grad_out.1), custom_call_target="tpu_custom_call" | custom-call | flops 2147483648 | bytes 18874368 | tf_op jit(solution)/shard_map/gather_project/pallas_call | solution.py:671
  65.6 0.0 copy-done
  65.6 0.0 copy-done.1
  65.6 7.4 %attend.1 = (bf16[16,128,128]{2,1,0:T(8,128)(2,1)S(1)}, bf16[128,2048]{1,0:T(8,128)(2,1)S(1)}, f32[16,2,128,128]{3,2,1,0:T(8,128)S(1)}) custom-call(bf16[16,128,128]{2,1,0:T(8,128)(2,1)S(1)} %get-tuple-element.14.q, bf16[32,2,128,128]{3,2,1,0:T(8,128)(2,1)S(1)} %get-tuple-element.15.kv, bf16[16,128,128]{2,1,0:T(8,128)(2,1)S(1)} %get-tuple-element.16.cot, ...), custom_call_target="tpu_custom_call" | custom-call | flops 2013265920 | bytes 6291456 | tf_op jit(solution)/shard_map/attend/pallas_call | solution.py:708
  73.0 23.9 %scatter_grads.1 = (bf16[256,1024]{1,0:T(8,128)(2,1)S(1)}, f32[16,1024]{1,0:T(8,128)S(1)}, f32[16,1024]{1,0:T(8,128)S(1)}) custom-call(bf16[16,128,2048]{2,1,0:T(8,128)(2,1)S(1)} %get-tuple-element.13.feats, bf16[16,128,128]{2,1,0:T(8,128)(2,1)S(1)} %get-tuple-element.17.out_blocks, bf16[128,2048]{1,0:T(8,128)(2,1)S(1)} %get-tuple-element.18.dqt, ...), custom_call_target="tpu_custom_call" | custom-call | flops 2147483648 | bytes 12582912 | tf_op jit(solution)/shard_map/scatter_grads/pallas_call | solution.py:723
  96.9 0.9 place.1
Async XLA Ops:
  0.6 65.0 %copy-start = (s32[256,5]{0,1:T(8,128)S(1)}, s32[256,5]{0,1:T(8,128)}, u32[]{:S(2)}) copy-start(s32[256,5]{0,1:T(8,128)} %param.10) | copy-start | bytes 15364
  0.6 65.0 %copy-start.1 = (s32[256]{0:T(256)S(1)}, s32[256]{0:T(256)}, u32[]{:S(2)}) copy-start(s32[256]{0:T(256)} %col_count.1) | copy-start | bytes 3076

commit v5 on v4

--- a/solution.py
+++ b/solution.py
@@ -584,7 +584,7 @@
             fin_recv.at[t, clus % PER],
         )
 
-    for t in (0, 1):
+    def finish(t):
         for i in range(3, 7):
             z_copy(t, i).wait_recv()
         for k in range(PER):
@@ -606,20 +606,13 @@
             def _():
                 remote(src, dst, fin_send.at[t, k], recv, (to, fsdp, clus // PER)).start()
 
+    finish(0)
+
     give.wait_send()
     for t in (0, 1):
         half_copy(t).wait_send()
-        for i in range(7):
+        for i in range(5):
             z_copy(t, i).wait_send()
-
-
-        @pl.loop(0, PER)
-        def _(k):
-            to, src, dst, recv = fin_copy(t, k)
-
-            @pl.when(to != clus)
-            def _():
-                remote(src, dst, fin_send.at[t, k], recv, (to, fsdp, clus // PER)).wait_send()
 
     @pl.loop(0, NC)
     def _(s):
@@ -636,6 +629,22 @@
                 out_recv.at[2 * m + block],
                 sibling,
             ).wait_recv()
+
+    finish(1)
+
+    for t in (0, 1):
+        for i in (5, 6):
+            z_copy(t, i).wait_send()
+
+        @pl.loop(0, PER)
+        def _(k):
+            to, src, dst, recv = fin_copy(t, k)
+
+            @pl.when(to != clus)
+            def _():
+                remote(src, dst, fin_send.at[t, k], recv, (to, fsdp, clus // PER)).wait_send()
+
+    for m in range(PER):
         for t in (0, 1):
             remote(
                 fin.at[t, 0],

time: 97.9 us -> 97.9 us (level)
  no operation moved by 1% of the time
where the time goes in v5:
time: 97.9 us; the launch traced here: 97.8 us
  Pallas kernels  97.1 us (99%)
    pallas_call x1, Pallas kernels, on_device(): pl.pallas_call(gather_kernel, name='gather_project', out_shape=(shape((NC...  64.9 us
    pallas_call x1, Pallas kernels, on_device(): pl.pallas_call(scatter_kernel, name='scatter_grads', out_shape=(shape((2...  23.9 us
    pallas_call x1, Pallas kernels, on_device(): pl.pallas_call(attend_kernel, name='attend', out_shape=(shape((NC, BLK, H...  7.36 us

profile of v5, /device:TPU:1, one launch (start us, length us, event | category | flops | bytes accessed | tf_op | source)
XLA Modules:
  0.0 97.8 jit_solution(5777533467871232515)
XLA Ops:
  0.6 0.0 copy-start
  0.6 0.0 copy-start.1
  0.7 64.9 %gather_project.1 = (bf16[16,128,2048]{2,1,0:T(8,128)(2,1)S(1)}, bf16[16,128,128]{2,1,0:T(8,128)(2,1)S(1)}, bf16[32,2,128,128]{3,2,1,0:T(8,128)(2,1)S(1)}, bf16[16,128,128]{2,1,0:T(8,128)(2,1)S(1)}) custom-call(bf16[256,2048]{1,0:T(8,128)(2,1)} %feats.1, f32[16,1024]{1,0:T(8,128)} %w_query.1, f32[16,1024]{1,0:T(8,128)} %w_keyval.1, bf16[256,1024]{1,0:T(8,128)(2,1)} %grad_out.1), custom_call_target="tpu_custom_call" | custom-call | flops 2147483648 | bytes 18874368 | tf_op jit(solution)/shard_map/gather_project/pallas_call | solution.py:680
  65.6 0.0 copy-done
  65.6 0.0 copy-done.1
  65.6 7.4 %attend.1 = (bf16[16,128,128]{2,1,0:T(8,128)(2,1)S(1)}, bf16[128,2048]{1,0:T(8,128)(2,1)S(1)}, f32[16,2,128,128]{3,2,1,0:T(8,128)S(1)}) custom-call(bf16[16,128,128]{2,1,0:T(8,128)(2,1)S(1)} %get-tuple-element.14.q, bf16[32,2,128,128]{3,2,1,0:T(8,128)(2,1)S(1)} %get-tuple-element.15.kv, bf16[16,128,128]{2,1,0:T(8,128)(2,1)S(1)} %get-tuple-element.16.cot, ...), custom_call_target="tpu_custom_call" | custom-call | flops 2013265920 | bytes 6291456 | tf_op jit(solution)/shard_map/attend/pallas_call | solution.py:717
  73.0 23.9 %scatter_grads.1 = (bf16[256,1024]{1,0:T(8,128)(2,1)S(1)}, f32[16,1024]{1,0:T(8,128)S(1)}, f32[16,1024]{1,0:T(8,128)S(1)}) custom-call(bf16[16,128,2048]{2,1,0:T(8,128)(2,1)S(1)} %get-tuple-element.13.feats, bf16[16,128,128]{2,1,0:T(8,128)(2,1)S(1)} %get-tuple-element.17.out_blocks, bf16[128,2048]{1,0:T(8,128)(2,1)S(1)} %get-tuple-element.18.dqt, ...), custom_call_target="tpu_custom_call" | custom-call | flops 2147483648 | bytes 12582912 | tf_op jit(solution)/shard_map/scatter_grads/pallas_call | solution.py:732
  96.9 0.9 place.1
Async XLA Ops:
  0.6 65.0 %copy-start = (s32[256,5]{0,1:T(8,128)S(1)}, s32[256,5]{0,1:T(8,128)}, u32[]{:S(2)}) copy-start(s32[256,5]{0,1:T(8,128)} %param.10) | copy-start | bytes 15364
  0.6 65.0 %copy-start.1 = (s32[256]{0:T(256)S(1)}, s32[256]{0:T(256)}, u32[]{:S(2)}) copy-start(s32[256]{0:T(256)} %col_count.1) | copy-start | bytes 3076
